TPU v7x, 128 devices: a whole 4x4x4 slice. The times are simulated.
128 devices in a mesh: energy: 8 (over z, core), views: 16 (over y, x).
Axes of the slice: x: 4, y: 4, z: 4, core: 2. Of those that a mesh axis runs over, the one named last changes fastest.
Arguments:
- projector_tiles: float32 [64, 48, 128, 256], P('views'), may hold values from -0.0546875 to 0.0546875
- tile_blocks: int32 [64, 48], P('views'), may hold values from 0 to 255
- ray_counts: int32 [64], P('views'), may hold values from 64 to 128
- sinogram: float32 [64, 8192], P('energy', 'views'), may hold values from -6 to 6
- ray_weights: float32 [64, 8192], P('energy', 'views'), may hold values from 0.25 to 4
- start_volume: float32 [64, 65536], P('energy', 'views'), may hold values from -6 to 6
- split_target: float32 [16, 64, 4096], P('views', None, 'energy'), may hold values from -6 to 6
- scaled_dual: float32 [16, 64, 4096], P('views', None, 'energy'), may hold values from -3 to 3
Outputs:
- new_volume: float32 [64, 65536], P('energy', 'views')
- new_split: float32 [16, 64, 4096], P('views', None, 'energy')
- new_dual: float32 [16, 64, 4096], P('views', None, 'energy')
Inputs may be any that keep to these rules, and one draw needn't show every extreme that they name: `tile_blocks`: block indices may repeat within a ray block. `ray_counts`: rays of a block at or past its count are padding.
All inputs are finite; a program needn't handle non-finite values.
Results may differ from a plain program's by a relative error of at most 0.00022.
Values sent between devices are 32-bit elements; how exact they have to be, the bound alone decides.
A program may use at most 128 MiB of HBM per device.

v0:
```python
import jax
import jax.numpy as jnp
from jax import lax
from jax.sharding import PartitionSpec as P

PV = 64
ITERS = 3
PENALTY = 1.0
SHRINK = 16.0
exact_mode = lax.Precision.HIGHEST


def forward(gathered, projector_tiles, tile_blocks):
    channel_count = gathered.shape[0]
    block_voxels = projector_tiles.shape[3]
    block_grid = gathered.reshape(channel_count, -1, block_voxels)
    columns = block_grid[:, tile_blocks]
    projected = jnp.einsum("crtv,rtkv->crk", columns, projector_tiles, precision=exact_mode)
    return projected.reshape(channel_count, -1)


def backward(weighted, projector_tiles, tile_blocks, voxel_count):
    channel_count = weighted.shape[0]
    ray_blocks, per_block, ray_length, block_voxels = projector_tiles.shape
    ray_parts = weighted.reshape(channel_count, ray_blocks, ray_length)
    spread_rays = jnp.einsum("crk,rtkv->crtv", ray_parts, projector_tiles, precision=exact_mode)
    block_grid = jnp.zeros((channel_count, voxel_count // block_voxels, block_voxels), jnp.float32)
    block_grid = block_grid.at[:, tile_blocks.reshape(-1)].add(
        spread_rays.reshape(channel_count, ray_blocks * per_block, block_voxels)
    )
    return block_grid.reshape(channel_count, voxel_count)


def shrink_patches(merged):
    leading, channel_count, segment_len = merged.shape
    blocks = merged.reshape(channel_count, segment_len // PV, PV)
    gram_matrix = jnp.einsum("cpv,dpv->pcd", blocks, blocks, precision=exact_mode)
    shifted = gram_matrix + SHRINK * jnp.eye(channel_count, dtype=jnp.float32)
    factor = jnp.linalg.cholesky(shifted)
    right_side = jnp.transpose(blocks, (1, 0, 2))
    solved = jax.scipy.linalg.cho_solve((factor, True), right_side)
    shrunk = right_side - SHRINK * solved
    return jnp.transpose(shrunk, (1, 0, 2)).reshape(leading, channel_count, segment_len)


def local(
    projector_tiles,
    tile_blocks,
    ray_counts,
    sinogram,
    ray_weights,
    start_volume,
    split_target,
    scaled_dual,
):
    ray_length = projector_tiles.shape[2]
    live_rays = (
        lax.broadcasted_iota(jnp.int32, (ray_counts.shape[0], ray_length), 1) < ray_counts[:, None]
    ).astype(jnp.float32)
    ray_scale = ray_weights * live_rays.reshape(1, -1)
    target_shard = lax.all_to_all(
        split_target - scaled_dual, "energy", split_axis=1, concat_axis=2, tiled=True
    )[0]
    segment = target_shard.shape[1]
    voxel_count = segment * lax.axis_size("views")
    volume_now, target = (start_volume, target_shard)

    def normal_map(vector, measured, anchor):
        gathered = lax.all_gather(vector, "views", axis=1, tiled=True)
        weighted = ray_scale * (measured - forward(gathered, projector_tiles, tile_blocks))
        partial_sum = backward(weighted, projector_tiles, tile_blocks, voxel_count)
        summed = lax.psum_scatter(partial_sum, "views", scatter_dimension=1, tiled=True)
        return summed + PENALTY * (anchor - vector)

    residual = normal_map(volume_now, sinogram, target)

    def norm_total(vector):
        return lax.psum(jnp.sum(jnp.square(vector), axis=1), "views")

    direction = residual
    norm_now = norm_total(residual)
    for iteration in range(ITERS):
        mapped = -normal_map(direction, 0.0, 0.0)
        curvature = lax.psum(jnp.sum(direction * mapped, axis=1), "views")
        step_size = (norm_now / curvature)[:, None]
        volume_now = volume_now + step_size * direction
        if iteration + 1 < ITERS:
            residual = residual - step_size * mapped
            norm_next = norm_total(residual)
            direction = residual + (norm_next / norm_now)[:, None] * direction
            norm_now = norm_next
    volume_patch = lax.all_to_all(
        volume_now[None], "energy", split_axis=2, concat_axis=1, tiled=True
    )
    new_split = shrink_patches(volume_patch + scaled_dual)
    new_dual = scaled_dual + volume_patch - new_split
    return (volume_now, new_split, new_dual)


def solution(mesh):
    placed = (
        P("views", None, None, None),
        P("views", None),
        P("views"),
        P("energy", "views"),
        P("energy", "views"),
        P("energy", "views"),
        P("views", None, "energy"),
        P("views", None, "energy"),
    )
    return jax.shard_map(
        local,
        mesh=mesh,
        in_specs=placed,
        out_specs=(P("energy", "views"), P("views", None, "energy"), P("views", None, "energy")),
        check_vma=False,
    )
```

profile of v0, /device:TPU:1, one launch (start us, length us, event | category | flops | bytes accessed | tf_op | source)
XLA Modules:
  0.0 1047.2 jit_solution(1356048474511867620)
XLA Ops:
  10.2 47.1 %all-gather.5.cloned.1.call-done = f32[8,65536]{1,0:T(8,128)} async-done(((f32[8,4096]{1,0:T(8,128)}), f32[8,65536]{1,0:T(8,128)}) %all-gather.5.cloned.1.call-update) | async-done | bytes 2097168 | tf_op jit(solution)/shard_map/all_gather | solution.py:69
  59.7 24.1 %fusion.16 = f32[8,4,128,1]{2,0,3,1:T(8,128)S(1)} fusion(f32[8,512]{1,0:T(8,128)S(1)} %copy-done.14, f32[8,4,48,256]{3,0,2,1:T(8,128)S(1)} %bitcast.197, f32[4,48,128,256]{3,2,1,0:T(8,128)} %param.8, f32[8,512]{1,0:T(8,128)S(1)} %copy-done.12, f32[512]{0:T(512)S(1)} %convert_bitcast_fusion), kind=kOutput, calls=%fused_computation.29 | convolution fusion | flops 603992064 | bytes 26789888 | tf_op jit(solution)/shard_map/crtv,rtkv->crk/dot_general | solution.py:18
  125.0 61.7 %reduce-scatter.5.cloned.1.call-done = f32[8,4096]{1,0:T(8,128)} async-done(((f32[8,65536]{1,0:T(8,128)}), f32[8,4096]{1,0:T(8,128)}) %reduce-scatter.5.cloned.1.call-update) | async-done | bytes 131088 | tf_op jit(solution)/shard_map/reduce_scatter | solution.py:72
  188.6 46.1 %all-gather.7.cloned.1.call-done = f32[8,65536]{1,0:T(8,128)} async-done(((f32[8,4096]{1,0:T(8,128)}), f32[8,65536]{1,0:T(8,128)}) %all-gather.7.cloned.1.call-update) | async-done | bytes 2097168 | tf_op jit(solution)/shard_map/all_gather | solution.py:69
  236.9 22.7 %fusion.13 = f32[8,4,128,1]{2,0,3,1:T(8,128)S(1)} fusion(f32[8,4,48,256]{3,0,2,1:T(8,128)S(1)} %bitcast.195, f32[4,48,128,256]{3,2,1,0:T(8,128)} %param.8, f32[8,512]{1,0:T(8,128)S(1)} %copy-done.12, f32[512]{0:T(512)S(1)} %convert_bitcast_fusion), kind=kOutput, calls=%fused_computation.25 | convolution fusion | flops 603992064 | bytes 26773504 | tf_op jit(solution)/shard_map/crtv,rtkv->crk/dot_general | solution.py:18
  259.6 15.8 %fusion.27 = f32[4,8,48,256]{3,1,2,0:T(8,128)} fusion(f32[8,4,128,1]{2,0,3,1:T(8,128)S(1)} %fusion.13, f32[4,48,128,256]{3,2,1,0:T(8,128)} %param.8), kind=kOutput, calls=%fused_computation.68 | convolution fusion | flops 603979776 | bytes 26755072 | tf_op jit(solution)/shard_map/crk,rtkv->crtv/dot_general | solution.py:26
  292.4 72.9 %reduce-scatter.7.cloned.1.call-done = f32[8,4096]{1,0:T(8,128)} async-done(((f32[8,65536]{1,0:T(8,128)}), f32[8,4096]{1,0:T(8,128)}) %reduce-scatter.7.cloned.1.call-update) | async-done | bytes 131088 | tf_op jit(solution)/shard_map/reduce_scatter | solution.py:72
  366.4 30.9 %all-reduce = (f32[8]{0:T(128)S(1)}, f32[8]{0:T(128)S(1)}) all-reduce(f32[8]{0:T(128)S(1)} %get-tuple-element.7, f32[8]{0:T(128)S(1)} %get-tuple-element.6), channel_id=1, replica_groups=mesh['energy'=8,'views'=16] {'views'}, use_global_device_ids=true, to_apply=%region_3.0 | all-reduce | flops 16 | bytes 128 | tf_op jit(solution)/shard_map/psum | solution.py:78
  398.4 28.5 %psum.44 = f32[8]{0:T(128)S(1)} all-reduce(f32[8]{0:T(128)S(1)} %get-tuple-element.10), channel_id=1, replica_groups=mesh['energy'=8,'views'=16] {'views'}, use_global_device_ids=true, to_apply=%region_9.0 | all-reduce | flops 8 | bytes 64 | tf_op jit(solution)/shard_map/psum | solution.py:78
  428.0 57.6 %all-gather.9.cloned.1.call-done = f32[8,65536]{1,0:T(8,128)} async-done(((f32[8,4096]{1,0:T(8,128)}), f32[8,65536]{1,0:T(8,128)}) %all-gather.9.cloned.1.call-update) | async-done | bytes 2097168 | tf_op jit(solution)/shard_map/all_gather | solution.py:69
  487.8 22.7 %fusion.9 = f32[8,4,128,1]{2,0,3,1:T(8,128)S(1)} fusion(f32[8,4,48,256]{3,0,2,1:T(8,128)S(1)} %bitcast.196, f32[4,48,128,256]{3,2,1,0:T(8,128)} %param.8, f32[8,512]{1,0:T(8,128)S(1)} %copy-done.12, f32[512]{0:T(512)S(1)} %convert_bitcast_fusion), kind=kOutput, calls=%fused_computation.20 | convolution fusion | flops 603992064 | bytes 26773504 | tf_op jit(solution)/shard_map/crtv,rtkv->crk/dot_general | solution.py:18
  510.5 15.8 %fusion.28 = f32[4,8,48,256]{3,1,2,0:T(8,128)} fusion(f32[8,4,128,1]{2,0,3,1:T(8,128)S(1)} %fusion.9, f32[4,48,128,256]{3,2,1,0:T(8,128)} %param.8), kind=kOutput, calls=%fused_computation.69 | convolution fusion | flops 603979776 | bytes 26755072 | tf_op jit(solution)/shard_map/crk,rtkv->crtv/dot_general | solution.py:26
  526.4 15.5 %scatter_fusion.2 = f32[8,256,256]{2,0,1:T(8,128)S(1)} fusion(f32[8,256,256]{2,0,1:T(8,128)S(1)} %broadcast.144.clone.2, s32[192]{0:T(256)S(1)} %bitcast.208, f32[192,8,256]{2,1,0:T(8,128)} %bitcast.193), kind=kCustom, calls=%fused_computation.6 | custom fusion | flops 393216 | bytes 4719360 | tf_op jit(solution)/shard_map/scatter-add | solution.py:28
  543.3 72.9 %reduce-scatter.9.cloned.1.call-done = f32[8,4096]{1,0:T(8,128)} async-done(((f32[8,65536]{1,0:T(8,128)}), f32[8,4096]{1,0:T(8,128)}) %reduce-scatter.9.cloned.1.call-update) | async-done | bytes 131088 | tf_op jit(solution)/shard_map/reduce_scatter | solution.py:72
  617.3 30.9 %psum.45 = f32[8]{0:T(128)S(1)} all-reduce(f32[8]{0:T(128)S(1)} %multiply_reduce_fusion.2), channel_id=1, replica_groups=mesh['energy'=8,'views'=16] {'views'}, use_global_device_ids=true, to_apply=%region_13.0 | all-reduce | flops 8 | bytes 64 | tf_op jit(solution)/shard_map/psum | solution.py:84
  649.3 28.5 %psum.46 = f32[8]{0:T(128)S(1)} all-reduce(f32[8]{0:T(128)S(1)} %multiply_reduce_fusion.1), channel_id=1, replica_groups=mesh['energy'=8,'views'=16] {'views'}, use_global_device_ids=true, to_apply=%region_15.0 | all-reduce | flops 8 | bytes 64 | tf_op jit(solution)/shard_map/psum | solution.py:78
  679.8 57.5 %all-gather.11.cloned.1.call-done = f32[8,65536]{1,0:T(8,128)} async-done(((f32[8,4096]{1,0:T(8,128)}), f32[8,65536]{1,0:T(8,128)}) %all-gather.11.cloned.1.call-update) | async-done | bytes 2097168 | tf_op jit(solution)/shard_map/all_gather | solution.py:69
  739.6 22.7 %fusion.5 = f32[8,4,128,1]{2,0,3,1:T(8,128)S(1)} fusion(f32[8,4,48,256]{3,0,2,1:T(8,128)S(1)} %bitcast.194, f32[4,48,128,256]{3,2,1,0:T(8,128)} %param.8, f32[8,512]{1,0:T(8,128)S(1)} %copy-done.12, f32[512]{0:T(512)S(1)} %convert_bitcast_fusion), kind=kOutput, calls=%fused_computation.15 | convolution fusion | flops 603992064 | bytes 26773504 | tf_op jit(solution)/shard_map/crtv,rtkv->crk/dot_general | solution.py:18
  762.3 15.8 %fusion.29 = f32[4,8,48,256]{3,1,2,0:T(8,128)} fusion(f32[8,4,128,1]{2,0,3,1:T(8,128)S(1)} %fusion.5, f32[4,48,128,256]{3,2,1,0:T(8,128)} %param.8), kind=kOutput, calls=%fused_computation.70 | convolution fusion | flops 603979776 | bytes 26755072 | tf_op jit(solution)/shard_map/crk,rtkv->crtv/dot_general | solution.py:26
  795.1 73.0 %reduce-scatter.11.cloned.1.call-done = f32[8,4096]{1,0:T(8,128)} async-done(((f32[8,65536]{1,0:T(8,128)}), f32[8,4096]{1,0:T(8,128)}) %reduce-scatter.11.cloned.1.call-update) | async-done | bytes 131088 | tf_op jit(solution)/shard_map/reduce_scatter | solution.py:72
  869.1 31.3 %psum.47 = f32[8]{0:T(128)S(1)} all-reduce(f32[8]{0:T(128)S(1)} %multiply_reduce_fusion), channel_id=1, replica_groups=mesh['energy'=8,'views'=16] {'views'}, use_global_device_ids=true, to_apply=%region_19.0 | all-reduce | flops 8 | bytes 64 | tf_op jit(solution)/shard_map/psum | solution.py:84
  903.6 19.4 %reduce.6 = f32[4096,8]{1,0:T(8,128)} reduce(f32[4096,1,8]{2,1,0:T(1,128)S(1)} %bitcast.188, f32[]{:T(128)} %broadcast.181), dimensions={1}, to_apply=%bitcast.165.reduce_sub_computation | reduce | bytes 262148
  951.6 46.9 %custom-call.11 = f32[8,64,64]{2,1,0:T(8,128)S(1)} custom-call(f32[8,64,64]{2,1,0:T(8,128)S(1)} %fusion.21), custom_call_target="Cholesky" | custom-call | tf_op jit(solution)/shard_map/jit(cholesky)/cholesky | solution.py:39
  998.8 39.3 %custom-call.12 = f32[8,1,64,64]{2,3,1,0:T(8,128)S(1)} custom-call(f32[8,1,64,64]{3,2,1,0:T(8,128)S(1)} %select_bitcast_fusion), custom_call_target="InvertDiagBlocksLowerTriangular" | custom-call | tf_op jit(solution)/shard_map/jit(_cho_solve)/vmap()/triangular_solve | solution.py:41
  (106 shorter events, 133.0 us)
Async XLA Ops:
  7.2 52.5 %copy-start.14 = (f32[8,512]{1,0:T(8,128)S(1)}, f32[8,512]{1,0:T(8,128)}, u32[]{:S(2)}) copy-start(f32[8,512]{1,0:T(8,128)} %param.11) | copy-start | bytes 49156
  7.2 52.5 %copy-start.12 = (f32[8,512]{1,0:T(8,128)S(1)}, f32[8,512]{1,0:T(8,128)}, u32[]{:S(2)}) copy-start(f32[8,512]{1,0:T(8,128)} %param.12) | copy-start | bytes 49156
  7.2 50.2 %all-gather.5.cloned.1.call-start = ((), (), s32[]{:S(2)}) async-start(), calls=%async_computation.6 | async-start | bytes 2228224 | tf_op jit(solution)/shard_map/all_gather | solution.py:69
  7.9 178.8 %reduce-scatter.5.cloned.1.call-start = ((), (), s32[]{:S(2)}) async-start(), calls=%async_computation.7 | async-start | bytes 2228224 | tf_op jit(solution)/shard_map/reduce_scatter | solution.py:72
  59.7 24.2 %copy-start = (f32[4,48,128,256]{3,2,1,0:T(8,128)S(1)}, f32[4,48,128,256]{3,2,1,0:T(8,128)}, u32[]{:S(2)}) copy-start(f32[4,48,128,256]{3,2,1,0:T(8,128)} %param.8) | copy-start | bytes 75497472
  112.4 1.4 copy-start.2
  112.4 1.4 copy-start.9
  112.4 1.4 copy-start.13
  112.4 74.3 %copy-start.8 = (f32[8,4096]{1,0:T(8,128)S(1)}, f32[8,4096]{1,0:T(8,128)}, u32[]{:S(2)}) copy-start(f32[8,4096]{1,0:T(8,128)} %param.13) | copy-start | bytes 393220
  113.8 120.9 %all-gather.7.cloned.1.call-start = ((), (), s32[]{:S(2)}) async-start(), calls=%async_computation.8 | async-start | bytes 2228224 | tf_op jit(solution)/shard_map/all_gather | solution.py:69
  188.3 177.0 %reduce-scatter.7.cloned.1.call-start = ((), (), s32[]{:S(2)}) async-start(), calls=%async_computation.9 | async-start | bytes 2228224 | tf_op jit(solution)/shard_map/reduce_scatter | solution.py:72
  291.0 1.4 copy-start.3
  291.0 74.3 %copy-start.5 = (f32[8,4096]{1,0:T(8,128)S(1)}, f32[8,4096]{1,0:T(8,128)}, u32[]{:S(2)}) copy-start(f32[8,4096]{1,0:T(8,128)} %subtract_add_fusion) | copy-start | bytes 393220
  292.4 193.2 %all-gather.9.cloned.1.call-start = ((), (), s32[]{:S(2)}) async-start(), calls=%async_computation.10 | async-start | bytes 2228224 | tf_op jit(solution)/shard_map/all_gather | solution.py:69
  427.7 188.5 %reduce-scatter.9.cloned.1.call-start = ((), (), s32[]{:S(2)}) async-start(), calls=%async_computation.11 | async-start | bytes 2228224 | tf_op jit(solution)/shard_map/reduce_scatter | solution.py:72
  541.9 1.4 copy-start.4
  541.9 74.3 %copy-start.6 = (f32[8,4096]{1,0:T(8,128)S(1)}, f32[8,4096]{1,0:T(8,128)}, u32[]{:S(2)}) copy-start(f32[8,4096]{1,0:T(8,128)} %multiply_add_fusion.2) | copy-start | bytes 393220
  543.3 194.0 %all-gather.11.cloned.1.call-start = ((), (), s32[]{:S(2)}) async-start(), calls=%async_computation.12 | async-start | bytes 2228224 | tf_op jit(solution)/shard_map/all_gather | solution.py:69
  679.5 188.5 %reduce-scatter.11.cloned.1.call-start = ((), (), s32[]{:S(2)}) async-start(), calls=%async_computation.13 | async-start | bytes 2228224 | tf_op jit(solution)/shard_map/reduce_scatter | solution.py:72
  793.7 1.4 copy-start.1
  793.7 74.3 %copy-start.7 = (f32[8,4096]{1,0:T(8,128)S(1)}, f32[8,4096]{1,0:T(8,128)}, u32[]{:S(2)}) copy-start(f32[8,4096]{1,0:T(8,128)} %multiply_add_fusion.1) | copy-start | bytes 393220
  900.6 22.4 %copy-start.11 = (f32[8,4096]{1,0:T(8,128)}, f32[8,4096]{1,0:T(8,128)S(1)}, u32[]{:S(2)}) copy-start(f32[8,4096]{1,0:T(8,128)S(1)} %multiply_add_fusion) | copy-start | bytes 393220
  926.3 19.4 %all-to-all-start.1 = ((f32[8,1,4096]{2,1,0:T(1,128)}), f32[8,1,4096]{2,1,0:T(1,128)S(1)}, u32[]{:S(2)}, u32[]{:S(2)}) async-start(f32[8,1,4096]{2,1,0:T(1,128)} %reshape.254), calls=%async_computation.5 | async-start | bytes 262144 | tf_op jit(solution)/shard_map/all_to_all | solution.py:92
  1039.4 0.7 copy-start.10
Sparse Core Ops, SparseCore 0:
  10.2 47.1 all-gather.4
  113.9 72.7 reduce-scatter.4
  189.7 44.9 all-gather.6
  292.5 72.7 reduce-scatter.6
  427.8 57.6 all-gather.8
  543.4 72.7 reduce-scatter.8
  679.6 57.6 all-gather.10
  795.2 72.7 reduce-scatter.10
where the time goes:
time: 1060 us; the launch traced here: 1050 us
  waiting for transfers between devices  495 us (47%)
  other arithmetic  180 us (17%)
  blocking collectives  161 us (15%)
  matrix products  154 us (15%)
  local copies, waits for them, and re-layouts  27 us (3%)
  starting transfers between devices  15.2 us (1%)
  between operations  14.7 us (1%)
    reduce_scatter x4, waiting for transfers between devices, normal_map(): lax.psum_scatter(partial_sum, 'views', scatter_dimension=1, tiled=True)  280 us
    all_gather x4, waiting for transfers between devices, normal_map(): gathered = lax.all_gather(vector, 'views', axis=1, tiled=True)  208 us
    dot_general x4, matrix products, forward(): jnp.einsum('crtv,rtkv->crk', columns, projector_tiles, precision=exact_mode)  92.2 us
    psum x3, blocking collectives, norm_total(): return lax.psum(jnp.sum(jnp.square(vector), axis=1), 'views')  87.9 us
    psum x2, blocking collectives, local(): curvature = lax.psum(jnp.sum(direction * mapped, axis=1), 'views')  62.2 us
    scatter-add x4, other arithmetic, backward(): block_grid.at[:, tile_blocks.reshape(-1)]  61.9 us
    dot_general x4, matrix products, backward(): jnp.einsum('crk,rtkv->crtv', ray_parts, projector_tiles, precision=exact_...  60.3 us
    another operation x4, other arithmetic, shrink_patches(): factor = jnp.linalg.cholesky(shifted)  47.1 us
  transfers between devices with their start and end apart: 9, of which 9 were waited for; matrix products, arithmetic and copies ran while one was open for 0% of the time, Pallas kernels for 0%

commit v1 on v0

--- a/solution.py
+++ b/solution.py
@@ -66,7 +66,9 @@
     volume_now, target = (start_volume, target_shard)
 
     def normal_map(vector, measured, anchor):
-        gathered = lax.all_gather(vector, "views", axis=1, tiled=True)
+        gathered = jnp.concatenate(
+            lax.all_to_all(jnp.stack([vector] * lax.axis_size("views")), "views", 0, 0), axis=1
+        )
         weighted = ray_scale * (measured - forward(gathered, projector_tiles, tile_blocks))
         partial_sum = backward(weighted, projector_tiles, tile_blocks, voxel_count)
         summed = lax.psum_scatter(partial_sum, "views", scatter_dimension=1, tiled=True)

time: 1060 us -> 988 us (0.932)
  waiting for transfers between devices: 495 us -> 348 us
  blocking collectives: 161 us -> 234 us
    all_gather x4 -> x0, waiting for transfers between devices: 208 us -> none  [normal_map(): gathered = lax.all_gather(vector, 'views', axis=1, tiled=True)]
    all_to_all x0 -> x3, blocking collectives: none -> 71 us  [normal_map(): lax.all_to_all(jnp.stack([vector] * lax.axis_size('views')), 'views', 0, 0)]
    reduce_scatter x4, waiting for transfers between devices: 280 us -> 313 us  [normal_map(): lax.psum_scatter(partial_sum, 'views', scatter_dimension=1, tiled=True)]
    all_to_all x0 -> x1, waiting for transfers between devices: none -> 30.1 us  [normal_map(): lax.all_to_all(jnp.stack([vector] * lax.axis_size('views')), 'views', 0, 0)]
  transfers between devices with their start and end apart: 9 -> 6, of which waited for: 9 -> 6; matrix products, arithmetic and copies ran while one was open for 0% -> 0% of each run, Pallas kernels for 0% -> 0%
where the time goes in v1:
time: 988 us; the launch traced here: 979 us
  waiting for transfers between devices  348 us (35%)
  blocking collectives  234 us (24%)
  other arithmetic  177 us (18%)
  matrix products  155 us (16%)
  local copies, waits for them, and re-layouts  28.4 us (3%)
  starting transfers between devices  22.1 us (2%)
  between operations  14.3 us (1%)
    reduce_scatter x4, waiting for transfers between devices, normal_map(): lax.psum_scatter(partial_sum, 'views', scatter_dimension=1, tiled=True)  313 us
    dot_general x4, matrix products, forward(): jnp.einsum('crtv,rtkv->crk', columns, projector_tiles, precision=exact_mode)  92.8 us
    psum x3, blocking collectives, norm_total(): return lax.psum(jnp.sum(jnp.square(vector), axis=1), 'views')  87.9 us
    all_to_all x3, blocking collectives, normal_map(): lax.all_to_all(jnp.stack([vector] * lax.axis_size('views')), 'views', 0, 0)  71 us
    psum x2, blocking collectives, local(): curvature = lax.psum(jnp.sum(direction * mapped, axis=1), 'views')  62.3 us
    scatter-add x4, other arithmetic, backward(): block_grid.at[:, tile_blocks.reshape(-1)]  61.9 us
    dot_general x4, matrix products, backward(): jnp.einsum('crk,rtkv->crtv', ray_parts, projector_tiles, precision=exact_...  60.3 us
    another operation x4, other arithmetic, shrink_patches(): factor = jnp.linalg.cholesky(shifted)  47.1 us
  transfers between devices with their start and end apart: 6, of which 6 were waited for; matrix products, arithmetic and copies ran while one was open for 0% of the time, Pallas kernels for 0%

profile of v1, /device:TPU:1, one launch (start us, length us, event | category | flops | bytes accessed | tf_op | source)
XLA Modules:
  0.0 978.6 jit_solution(11127223580994648104)
XLA Ops:
  17.7 30.1 %all-to-all-done = f32[16,8,4096]{2,1,0:T(8,128)S(1)} async-done(((f32[16,8,4096]{2,1,0:T(8,128)}), f32[16,8,4096]{2,1,0:T(8,128)S(1)}, u32[]{:S(2)}, u32[]{:S(2)}) %all-to-all-start) | async-done | bytes 2097184 | tf_op jit(solution)/shard_map/all_to_all | solution.py:70
  49.9 24.4 %fusion.16 = f32[8,4,128,1]{2,0,3,1:T(8,128)S(1)} fusion(f32[8,512]{1,0:T(8,128)S(1)} %copy-done.11, f32[8,4,48,256]{3,0,2,1:T(8,128)} %bitcast.209, f32[4,48,128,256]{3,2,1,0:T(8,128)} %param.8, f32[8,512]{1,0:T(8,128)S(1)} %copy-done.9, f32[512]{0:T(512)S(1)} %convert_bitcast_fusion), kind=kOutput, calls=%fused_computation.29 | convolution fusion | flops 603992064 | bytes 26789888 | tf_op jit(solution)/shard_map/crtv,rtkv->crk/dot_general | solution.py:18
  87.4 15.5 %scatter_fusion = f32[8,256,256]{2,0,1:T(8,128)S(1)} fusion(f32[8,256,256]{2,0,1:T(8,128)S(1)} %broadcast.152.clone, s32[192]{0:T(256)S(1)} %bitcast.214, f32[192,8,256]{2,1,0:T(8,128)} %bitcast.203), kind=kCustom, calls=%fused_computation.4 | custom fusion | flops 393216 | bytes 4719360 | tf_op jit(solution)/shard_map/scatter-add | solution.py:28
  117.0 60.3 %reduce-scatter.5.cloned.1.call-done = f32[8,4096]{1,0:T(8,128)} async-done(((f32[8,65536]{1,0:T(8,128)}), f32[8,4096]{1,0:T(8,128)}) %reduce-scatter.5.cloned.1.call-update) | async-done | bytes 131088 | tf_op jit(solution)/shard_map/reduce_scatter | solution.py:74
  178.4 29.9 %all_to_all.54 = f32[16,8,4096]{2,1,0:T(8,128)S(1)} all-to-all(f32[16,8,4096]{2,1,0:T(8,128)S(1)} %stack.9), channel_id=1, replica_groups=mesh['energy'=8,'views'=16] {'views'}, dimensions={0} | all-to-all | bytes 4194304 | tf_op jit(solution)/shard_map/all_to_all | solution.py:70
  210.3 22.8 %fusion.13 = f32[8,4,128,1]{2,0,3,1:T(8,128)S(1)} fusion(f32[8,4,48,256]{3,0,2,1:T(8,128)} %bitcast.207, f32[4,48,128,256]{3,2,1,0:T(8,128)} %param.8, f32[8,512]{1,0:T(8,128)S(1)} %copy-done.9, f32[512]{0:T(512)S(1)} %convert_bitcast_fusion), kind=kOutput, calls=%fused_computation.25 | convolution fusion | flops 603992064 | bytes 26773504 | tf_op jit(solution)/shard_map/crtv,rtkv->crk/dot_general | solution.py:18
  233.2 15.8 %fusion.27 = f32[4,8,48,256]{3,1,2,0:T(8,128)} fusion(f32[8,4,128,1]{2,0,3,1:T(8,128)S(1)} %fusion.13, f32[4,48,128,256]{3,2,1,0:T(8,128)} %param.8), kind=kOutput, calls=%fused_computation.68 | convolution fusion | flops 603979776 | bytes 26755072 | tf_op jit(solution)/shard_map/crk,rtkv->crtv/dot_general | solution.py:26
  266.0 73.5 %reduce-scatter.7.cloned.1.call-done = f32[8,4096]{1,0:T(8,128)} async-done(((f32[8,65536]{1,0:T(8,128)}), f32[8,4096]{1,0:T(8,128)}) %reduce-scatter.7.cloned.1.call-update) | async-done | bytes 131088 | tf_op jit(solution)/shard_map/reduce_scatter | solution.py:74
  340.6 30.9 %all-reduce = (f32[8]{0:T(128)S(1)}, f32[8]{0:T(128)S(1)}) all-reduce(f32[8]{0:T(128)S(1)} %get-tuple-element.7, f32[8]{0:T(128)S(1)} %get-tuple-element.6), channel_id=1, replica_groups=mesh['energy'=8,'views'=16] {'views'}, use_global_device_ids=true, to_apply=%region_3.0 | all-reduce | flops 16 | bytes 128 | tf_op jit(solution)/shard_map/psum | solution.py:80
  372.6 28.5 %psum.44 = f32[8]{0:T(128)S(1)} all-reduce(f32[8]{0:T(128)S(1)} %get-tuple-element.10), channel_id=1, replica_groups=mesh['energy'=8,'views'=16] {'views'}, use_global_device_ids=true, to_apply=%region_9.0 | all-reduce | flops 8 | bytes 64 | tf_op jit(solution)/shard_map/psum | solution.py:80
  401.4 20.5 %all_to_all.55 = f32[16,8,4096]{2,1,0:T(8,128)S(1)} all-to-all(f32[16,8,4096]{2,1,0:T(8,128)S(1)} %stack.10), channel_id=1, replica_groups=mesh['energy'=8,'views'=16] {'views'}, dimensions={0} | all-to-all | bytes 4194304 | tf_op jit(solution)/shard_map/all_to_all | solution.py:70
  424.0 22.8 %fusion.9 = f32[8,4,128,1]{2,0,3,1:T(8,128)S(1)} fusion(f32[8,4,48,256]{3,0,2,1:T(8,128)} %bitcast.208, f32[4,48,128,256]{3,2,1,0:T(8,128)} %param.8, f32[8,512]{1,0:T(8,128)S(1)} %copy-done.9, f32[512]{0:T(512)S(1)} %convert_bitcast_fusion), kind=kOutput, calls=%fused_computation.20 | convolution fusion | flops 603992064 | bytes 26773504 | tf_op jit(solution)/shard_map/crtv,rtkv->crk/dot_general | solution.py:18
  446.8 15.8 %fusion.28 = f32[4,8,48,256]{3,1,2,0:T(8,128)} fusion(f32[8,4,128,1]{2,0,3,1:T(8,128)S(1)} %fusion.9, f32[4,48,128,256]{3,2,1,0:T(8,128)} %param.8), kind=kOutput, calls=%fused_computation.69 | convolution fusion | flops 603979776 | bytes 26755072 | tf_op jit(solution)/shard_map/crk,rtkv->crtv/dot_general | solution.py:26
  479.6 90.1 %reduce-scatter.9.cloned.1.call-done = f32[8,4096]{1,0:T(8,128)} async-done(((f32[8,65536]{1,0:T(8,128)}), f32[8,4096]{1,0:T(8,128)}) %reduce-scatter.9.cloned.1.call-update) | async-done | bytes 131088 | tf_op jit(solution)/shard_map/reduce_scatter | solution.py:74
  570.8 30.9 %psum.45 = f32[8]{0:T(128)S(1)} all-reduce(f32[8]{0:T(128)S(1)} %multiply_reduce_fusion.2), channel_id=1, replica_groups=mesh['energy'=8,'views'=16] {'views'}, use_global_device_ids=true, to_apply=%region_13.0 | all-reduce | flops 8 | bytes 64 | tf_op jit(solution)/shard_map/psum | solution.py:86
  602.8 28.5 %psum.46 = f32[8]{0:T(128)S(1)} all-reduce(f32[8]{0:T(128)S(1)} %multiply_reduce_fusion.1), channel_id=1, replica_groups=mesh['energy'=8,'views'=16] {'views'}, use_global_device_ids=true, to_apply=%region_15.0 | all-reduce | flops 8 | bytes 64 | tf_op jit(solution)/shard_map/psum | solution.py:80
  632.5 20.6 %all_to_all.56 = f32[16,8,4096]{2,1,0:T(8,128)S(1)} all-to-all(f32[16,8,4096]{2,1,0:T(8,128)S(1)} %stack.11), channel_id=1, replica_groups=mesh['energy'=8,'views'=16] {'views'}, dimensions={0} | all-to-all | bytes 4194304 | tf_op jit(solution)/shard_map/all_to_all | solution.py:70
  655.2 22.8 %fusion.5 = f32[8,4,128,1]{2,0,3,1:T(8,128)S(1)} fusion(f32[8,4,48,256]{3,0,2,1:T(8,128)} %bitcast.206, f32[4,48,128,256]{3,2,1,0:T(8,128)} %param.8, f32[8,512]{1,0:T(8,128)S(1)} %copy-done.9, f32[512]{0:T(512)S(1)} %convert_bitcast_fusion), kind=kOutput, calls=%fused_computation.15 | convolution fusion | flops 603992064 | bytes 26773504 | tf_op jit(solution)/shard_map/crtv,rtkv->crk/dot_general | solution.py:18
  678.0 15.8 %fusion.29 = f32[4,8,48,256]{3,1,2,0:T(8,128)} fusion(f32[8,4,128,1]{2,0,3,1:T(8,128)S(1)} %fusion.5, f32[4,48,128,256]{3,2,1,0:T(8,128)} %param.8), kind=kOutput, calls=%fused_computation.70 | convolution fusion | flops 603979776 | bytes 26755072 | tf_op jit(solution)/shard_map/crk,rtkv->crtv/dot_general | solution.py:26
  710.7 89.0 %reduce-scatter.11.cloned.1.call-done = f32[8,4096]{1,0:T(8,128)} async-done(((f32[8,65536]{1,0:T(8,128)}), f32[8,4096]{1,0:T(8,128)}) %reduce-scatter.11.cloned.1.call-update) | async-done | bytes 131088 | tf_op jit(solution)/shard_map/reduce_scatter | solution.py:74
  800.8 31.4 %psum.47 = f32[8]{0:T(128)S(1)} all-reduce(f32[8]{0:T(128)S(1)} %multiply_reduce_fusion), channel_id=1, replica_groups=mesh['energy'=8,'views'=16] {'views'}, use_global_device_ids=true, to_apply=%region_19.0 | all-reduce | flops 8 | bytes 64 | tf_op jit(solution)/shard_map/psum | solution.py:86
  835.3 19.4 %reduce.6 = f32[4096,8]{1,0:T(8,128)} reduce(f32[4096,1,8]{2,1,0:T(1,128)S(1)} %bitcast.196, f32[]{:T(128)} %broadcast.189), dimensions={1}, to_apply=%bitcast.173.reduce_sub_computation | reduce | bytes 262148
  883.4 46.9 %custom-call.11 = f32[8,64,64]{2,1,0:T(8,128)S(1)} custom-call(f32[8,64,64]{2,1,0:T(8,128)S(1)} %fusion.21), custom_call_target="Cholesky" | custom-call | tf_op jit(solution)/shard_map/jit(cholesky)/cholesky | solution.py:39
  930.5 39.3 %custom-call.12 = f32[8,1,64,64]{2,3,1,0:T(8,128)S(1)} custom-call(f32[8,1,64,64]{3,2,1,0:T(8,128)S(1)} %select_bitcast_fusion), custom_call_target="InvertDiagBlocksLowerTriangular" | custom-call | tf_op jit(solution)/shard_map/jit(_cho_solve)/vmap()/triangular_solve | solution.py:41
  (101 shorter events, 138.8 us)
Async XLA Ops:
  9.6 7.8 copy-start.12
  9.6 8.0 copy-start.13
  9.6 38.2 %all-to-all-start = ((f32[16,8,4096]{2,1,0:T(8,128)}), f32[16,8,4096]{2,1,0:T(8,128)S(1)}, u32[]{:S(2)}, u32[]{:S(2)}) async-start(f32[16,8,4096]{2,1,0:T(8,128)} %stack.8), calls=%async_computation | async-start | bytes 4194304 | tf_op jit(solution)/shard_map/all_to_all | solution.py:70
  17.4 32.5 %copy-start.9 = (f32[8,512]{1,0:T(8,128)S(1)}, f32[8,512]{1,0:T(8,128)}, u32[]{:S(2)}) copy-start(f32[8,512]{1,0:T(8,128)} %param.12) | copy-start | bytes 49156
  17.4 32.5 %copy-start.11 = (f32[8,512]{1,0:T(8,128)S(1)}, f32[8,512]{1,0:T(8,128)}, u32[]{:S(2)}) copy-start(f32[8,512]{1,0:T(8,128)} %param.11) | copy-start | bytes 49156
  17.4 159.9 %reduce-scatter.5.cloned.1.call-start = ((), (), s32[]{:S(2)}) async-start(), calls=%async_computation.10 | async-start | bytes 2228224 | tf_op jit(solution)/shard_map/reduce_scatter | solution.py:74
  49.9 24.4 %copy-start = (f32[4,48,128,256]{3,2,1,0:T(8,128)S(1)}, f32[4,48,128,256]{3,2,1,0:T(8,128)}, u32[]{:S(2)}) copy-start(f32[4,48,128,256]{3,2,1,0:T(8,128)} %param.8) | copy-start | bytes 75497472
  102.8 1.4 copy-start.2
  102.9 1.4 copy-start.6
  102.9 1.4 copy-start.10
  102.9 74.4 %copy-start.5 = (f32[8,4096]{1,0:T(8,128)S(1)}, f32[8,4096]{1,0:T(8,128)}, u32[]{:S(2)}) copy-start(f32[8,4096]{1,0:T(8,128)} %param.13) | copy-start | bytes 393220
  104.2 235.3 %reduce-scatter.7.cloned.1.call-start = ((), (), s32[]{:S(2)}) async-start(), calls=%async_computation.11 | async-start | bytes 2228224 | tf_op jit(solution)/shard_map/reduce_scatter | solution.py:74
  264.6 1.4 copy-start.3
  265.9 303.8 %reduce-scatter.9.cloned.1.call-start = ((), (), s32[]{:S(2)}) async-start(), calls=%async_computation.12 | async-start | bytes 2228224 | tf_op jit(solution)/shard_map/reduce_scatter | solution.py:74
  478.2 1.4 copy-start.4
  479.6 320.2 %reduce-scatter.11.cloned.1.call-start = ((), (), s32[]{:S(2)}) async-start(), calls=%async_computation.13 | async-start | bytes 2228224 | tf_op jit(solution)/shard_map/reduce_scatter | solution.py:74
  709.4 1.4 copy-start.1
  832.3 22.4 %copy-start.8 = (f32[8,4096]{1,0:T(8,128)}, f32[8,4096]{1,0:T(8,128)S(1)}, u32[]{:S(2)}) copy-start(f32[8,4096]{1,0:T(8,128)S(1)} %multiply_add_fusion) | copy-start | bytes 393220
  858.0 19.4 %all-to-all-start.5 = ((f32[8,1,4096]{2,1,0:T(1,128)}), f32[8,1,4096]{2,1,0:T(1,128)S(1)}, u32[]{:S(2)}, u32[]{:S(2)}) async-start(f32[8,1,4096]{2,1,0:T(1,128)} %reshape.262), calls=%async_computation.9 | async-start | bytes 262144 | tf_op jit(solution)/shard_map/all_to_all | solution.py:94
  971.2 0.7 copy-start.7
Sparse Core Ops, SparseCore 0:
  104.3 72.9 reduce-scatter.4
  266.1 73.3 reduce-scatter.6
  479.7 89.9 reduce-scatter.8
  710.9 88.8 reduce-scatter.10
